TPU v7x, 32 devices: a whole 2x2x4 slice. The times are simulated.
32 devices in a mesh: dp: 4 (over z), sp: 8 (over y, x, core).
Axes of the slice: x: 2, y: 2, z: 4, core: 2. Of those that a mesh axis runs over, the one named last changes fastest.
Arguments:
- tokens: bfloat16 [4096, 2048], P(('dp', 'sp')), may hold values from -6 to 6
- doc_lengths: int32 [4, 4], P('dp'), may hold values from 1 to 1020, as said below
- w_query: bfloat16 [2048, 2048], P('sp'), may hold values from -0.15625 to 0.15625
- w_key: bfloat16 [2048, 512], P('sp'), may hold values from -0.15625 to 0.15625
- w_value: bfloat16 [2048, 512], P('sp'), may hold values from -0.125 to 0.125
- w_out: bfloat16 [2048, 2048], P('sp'), may hold values from -0.75 to 0.75
- gain_attn: bfloat16 [2048], P('sp'), may hold values from 0.5 to 1.5
- gain_mlp: bfloat16 [2048], P('sp'), may hold values from 0.5 to 1.5
- w_gate: bfloat16 [2048, 8192], P(None, 'sp'), may hold values from -0.125 to 0.125
- w_up: bfloat16 [2048, 8192], P(None, 'sp'), may hold values from -0.125 to 0.125
- w_down: bfloat16 [8192, 2048], P('sp'), may hold values from -0.0625 to 0.0625
- cotangent: bfloat16 [4096, 2048], P(('dp', 'sp')), may hold values from -6 to 6
Outputs:
- layer_out: bfloat16 [4096, 2048], P(('dp', 'sp'))
- grad_tokens: float32 [4096, 2048], P(('dp', 'sp'))
- grad_query: float32 [2048, 2048], P('sp')
- grad_key: float32 [2048, 512], P('sp')
- grad_value: float32 [2048, 512], P('sp')
- grad_out: float32 [2048, 2048], P('sp')
- grad_gain_attn: float32 [2048], P('sp')
- grad_gain_mlp: float32 [2048], P('sp')
- grad_gate: float32 [2048, 8192], P(None, 'sp')
- grad_up: float32 [2048, 8192], P(None, 'sp')
- grad_down: float32 [8192, 2048], P('sp')
Inputs may be any that keep to these rules, and one draw needn't show every extreme that they name: `doc_lengths`: each row gives the lengths of the 4 documents packed in order into one micro-batch of 1024 tokens; a row sums to 1024.
All inputs are finite; a program needn't handle non-finite values.
Results may differ from a plain program's by a relative error of at most 0.022.
Values may be sent and summed in bfloat16 or wider, within the bound.
No kernel may reach another device: no remote copies, remote signals or barrier semaphores. Data moves between devices by JAX's collectives and lax.ppermute only.
A program may use at most 192 MiB of HBM per device.

v0:
```python
import jax
import jax.numpy as jnp
from jax import lax
from jax.sharding import PartitionSpec as P

HD = 64
BLOCK = 512


EPS = 1e-05
THETA = 500000.0
FACTOR = 32.0
LOW_FACTOR = 1.0
HIGH_FACTOR = 4.0
BASE_CONTEXT = 8192.0
MASKED = -1e30


def frequencies(head_size):
    half_index = jnp.arange(head_size // 2).astype(jnp.float32)
    inverse = THETA ** (-2.0 * half_index / head_size)
    wavelength = 2.0 * jnp.pi / inverse
    smooth = (BASE_CONTEXT / wavelength - LOW_FACTOR) / (HIGH_FACTOR - LOW_FACTOR)
    middle = (1.0 - smooth) * inverse / FACTOR + smooth * inverse
    slow_band = jnp.where(wavelength > BASE_CONTEXT / LOW_FACTOR, inverse / FACTOR, middle)
    return jnp.where(wavelength < BASE_CONTEXT / HIGH_FACTOR, inverse, slow_band)


def doc_layout(lengths, first_row, row_total):
    ends_at = jnp.cumsum(lengths)
    starts_at = ends_at - lengths
    places = first_row + jnp.arange(row_total, dtype=jnp.int32)
    documents = jnp.sum((places[:, None] >= ends_at[None, :]).astype(jnp.int32), axis=1)
    begins = jnp.max(
        jnp.where(starts_at[None, :] <= places[:, None], starts_at[None, :], 0), axis=1
    )
    return (documents, places, places - begins)


def rotation(positions, head_size):
    angles = positions.astype(jnp.float32)[:, None] * frequencies(head_size)[None, :]
    cosine_table = jnp.concatenate([jnp.cos(angles), jnp.cos(angles)], axis=1)
    sine_table = jnp.concatenate([jnp.sin(angles), jnp.sin(angles)], axis=1)
    return (cosine_table, sine_table)


def rotate_half(values):
    middle = values.shape[-1] // 2
    return jnp.concatenate([-values[..., middle:], values[..., :middle]], axis=-1)


def apply_rope(values, cosine_table, sine_table):
    return values * cosine_table[:, None, :] + rotate_half(values) * sine_table[:, None, :]


def rope_back(gradients, cosine_table, sine_table):
    return gradients * cosine_table[:, None, :] - rotate_half(gradients) * sine_table[:, None, :]


def contract(left, right, left_dim, right_dim):
    return lax.dot_general(
        left, right, (((left_dim,), (right_dim,)), ((), ())), preferred_element_type=jnp.float32
    )


def block_rows(array, documents, block_index, heads):
    first_row = block_index * BLOCK
    row_block = lax.dynamic_slice_in_dim(array, first_row, BLOCK, 0).reshape(BLOCK, heads, HD)
    block_docs = lax.dynamic_slice_in_dim(documents, first_row, BLOCK, 0)
    places = first_row + jnp.arange(BLOCK, dtype=jnp.int32)
    return (row_block, block_docs, places)


def masked_scores(
    query_block, key_wide, query_docs, key_docs, query_places, key_places, score_scale
):
    scores = (
        jnp.einsum("qhd,khd->hqk", query_block, key_wide, preferred_element_type=jnp.float32)
        * score_scale
    )
    allowed = (query_docs[:, None] == key_docs[None, :]) & (
        key_places[None, :] <= query_places[:, None]
    )
    return jnp.where(allowed[None], scores, MASKED)


def add_block(whole, piece, block_index):
    current = lax.dynamic_slice_in_dim(whole, block_index * BLOCK, BLOCK, 0)
    return lax.dynamic_update_slice_in_dim(whole, current + piece, block_index * BLOCK, 0)


def attend(query_heads, key_heads, value_heads, documents, score_scale):
    total_rows = query_heads.shape[0]
    local_heads = query_heads.shape[1] // HD
    local_kv = key_heads.shape[1] // HD
    repeats = local_heads // local_kv
    blocks = total_rows // BLOCK

    def query_loop(block_index, carried):
        outputs, log_sums = carried
        query_block, query_docs, query_places = block_rows(
            query_heads, documents, block_index, local_heads
        )

        def scores_at(key_index):
            key_block, key_docs, key_places = block_rows(key_heads, documents, key_index, local_kv)
            return masked_scores(
                query_block,
                jnp.repeat(key_block, repeats, axis=1),
                query_docs,
                key_docs,
                query_places,
                key_places,
                score_scale,
            )

        def first_pass(key_index, running):
            running_max, running_sum = running
            scores = scores_at(key_index)
            new_max = jnp.maximum(running_max, jnp.max(scores, axis=2))
            running_sum = running_sum * jnp.exp(running_max - new_max) + jnp.sum(
                jnp.exp(scores - new_max[:, :, None]), axis=2
            )
            return (new_max, running_sum)

        initial = (
            jnp.full((local_heads, BLOCK), MASKED, jnp.float32),
            jnp.zeros((local_heads, BLOCK), jnp.float32),
        )
        running_max, running_sum = lax.fori_loop(0, block_index + 1, first_pass, initial)
        log_sum = running_max + jnp.log(running_sum)

        def second_pass(key_index, accumulated):
            value_block, _, _ = block_rows(value_heads, documents, key_index, local_kv)
            block_probs = jnp.exp(scores_at(key_index) - log_sum[:, :, None]).astype(jnp.bfloat16)
            return accumulated + jnp.einsum(
                "hqk,khd->qhd",
                block_probs,
                jnp.repeat(value_block, repeats, axis=1),
                preferred_element_type=jnp.float32,
            )

        block_out = lax.fori_loop(
            0, block_index + 1, second_pass, jnp.zeros((BLOCK, local_heads, HD), jnp.float32)
        )
        outputs = lax.dynamic_update_slice_in_dim(
            outputs,
            block_out.reshape(BLOCK, local_heads * HD).astype(jnp.bfloat16),
            block_index * BLOCK,
            0,
        )
        log_sums = lax.dynamic_update_slice_in_dim(log_sums, log_sum, block_index * BLOCK, 1)
        return (outputs, log_sums)

    initial = (
        jnp.zeros((total_rows, local_heads * HD), jnp.bfloat16),
        jnp.zeros((local_heads, total_rows), jnp.float32),
    )
    return lax.fori_loop(0, blocks, query_loop, initial)


def attend_back(query_heads, key_heads, value_heads, heads_back, log_sums, documents, score_scale):
    total_rows = query_heads.shape[0]
    local_heads = query_heads.shape[1] // HD
    local_kv = key_heads.shape[1] // HD
    repeats = local_heads // local_kv
    blocks = total_rows // BLOCK

    def query_loop(block_index, carried):
        query_grads, key_grads, value_grads = carried
        query_block, query_docs, query_places = block_rows(
            query_heads, documents, block_index, local_heads
        )
        back_block, _, _ = block_rows(heads_back, documents, block_index, local_heads)
        log_sum = lax.dynamic_slice_in_dim(log_sums, block_index * BLOCK, BLOCK, 1)

        def probs_at(key_index):
            key_block, key_docs, key_places = block_rows(key_heads, documents, key_index, local_kv)
            value_block, _, _ = block_rows(value_heads, documents, key_index, local_kv)
            key_wide = jnp.repeat(key_block, repeats, axis=1)
            value_wide = jnp.repeat(value_block, repeats, axis=1)
            scores = masked_scores(
                query_block, key_wide, query_docs, key_docs, query_places, key_places, score_scale
            )
            block_probs = jnp.exp(scores - log_sum[:, :, None])
            probs_back = jnp.einsum(
                "qhd,khd->hqk", back_block, value_wide, preferred_element_type=jnp.float32
            )
            return (block_probs, probs_back, key_wide)

        def delta_pass(key_index, accumulated):
            block_probs, probs_back, _ = probs_at(key_index)
            return accumulated + jnp.sum(block_probs * probs_back, axis=2)

        delta = lax.fori_loop(
            0, block_index + 1, delta_pass, jnp.zeros((local_heads, BLOCK), jnp.float32)
        )

        def grad_pass(key_index, inner):
            query_sum, key_whole, value_whole = inner
            block_probs, probs_back, key_wide = probs_at(key_index)
            scores_back = (block_probs * (probs_back - delta[:, :, None])).astype(jnp.bfloat16)
            query_sum = (
                query_sum
                + jnp.einsum(
                    "hqk,khd->qhd", scores_back, key_wide, preferred_element_type=jnp.float32
                )
                * score_scale
            )
            key_piece = (
                jnp.einsum(
                    "hqk,qhd->khd", scores_back, query_block, preferred_element_type=jnp.float32
                )
                * score_scale
            )
            value_piece = jnp.einsum(
                "hqk,qhd->khd",
                block_probs.astype(jnp.bfloat16),
                back_block,
                preferred_element_type=jnp.float32,
            )
            key_whole = add_block(
                key_whole, key_piece.reshape(BLOCK, local_kv, repeats, HD).sum(axis=2), key_index
            )
            value_whole = add_block(
                value_whole,
                value_piece.reshape(BLOCK, local_kv, repeats, HD).sum(axis=2),
                key_index,
            )
            return (query_sum, key_whole, value_whole)

        query_sum, key_grads, value_grads = lax.fori_loop(
            0,
            block_index + 1,
            grad_pass,
            (jnp.zeros((BLOCK, local_heads, HD), jnp.float32), key_grads, value_grads),
        )
        query_grads = lax.dynamic_update_slice_in_dim(
            query_grads,
            query_sum.reshape(BLOCK, local_heads * HD).astype(jnp.bfloat16),
            block_index * BLOCK,
            0,
        )
        return (query_grads, key_grads, value_grads)

    initial = (
        jnp.zeros((total_rows, local_heads * HD), jnp.bfloat16),
        jnp.zeros((total_rows, local_kv, HD), jnp.float32),
        jnp.zeros((total_rows, local_kv, HD), jnp.float32),
    )
    query_grads, key_grads, value_grads = lax.fori_loop(0, blocks, query_loop, initial)
    return (
        query_grads,
        key_grads.reshape(total_rows, local_kv * HD).astype(jnp.bfloat16),
        value_grads.reshape(total_rows, local_kv * HD).astype(jnp.bfloat16),
    )


def on_device(
    tokens,
    doc_lengths,
    w_query,
    w_key,
    w_value,
    w_out,
    gain_attn,
    gain_mlp,
    w_gate,
    w_up,
    w_down,
    cotangent,
):
    shards = lax.axis_size("sp")
    seq_rank = lax.axis_index("sp")
    tok_rows = tokens.shape[0]
    group_rows = tok_rows * shards
    full_query, full_key, full_value, full_out, full_gain_attn, full_gain_mlp = (
        lax.all_gather(w_query, "sp", axis=0, tiled=True),
        lax.all_gather(w_key, "sp", axis=0, tiled=True),
        lax.all_gather(w_value, "sp", axis=0, tiled=True),
        lax.all_gather(w_out, "sp", axis=0, tiled=True),
        lax.all_gather(gain_attn, "sp", axis=0, tiled=True),
        lax.all_gather(gain_mlp, "sp", axis=0, tiled=True),
    )
    heads_total = full_query.shape[1] // HD
    kv_total = full_key.shape[1] // HD
    copies = max(1, shards // kv_total)
    score_scale = HD ** (-0.5)
    lengths = doc_lengths[0]
    _, _, positions = doc_layout(lengths, seq_rank * tok_rows, tok_rows)
    cosine_table, sine_table = rotation(positions, HD)
    documents, _, _ = doc_layout(lengths, jnp.int32(0), group_rows)
    inputs = tokens.astype(jnp.float32)
    inverse_one = lax.rsqrt(jnp.mean(inputs * inputs, axis=1, keepdims=True) + EPS)
    normed_one = inputs * inverse_one
    gain_one = full_gain_attn.astype(jnp.float32)
    act_one = (normed_one * gain_one).astype(jnp.bfloat16)
    query_pre = jnp.dot(act_one, full_query, preferred_element_type=jnp.float32).reshape(
        tok_rows, heads_total, HD
    )
    key_pre = jnp.dot(act_one, full_key, preferred_element_type=jnp.float32).reshape(
        tok_rows, kv_total, HD
    )
    value_pre = jnp.dot(act_one, full_value, preferred_element_type=jnp.float32).reshape(
        tok_rows, kv_total, HD
    )
    query_rot = (
        apply_rope(query_pre, cosine_table, sine_table)
        .astype(jnp.bfloat16)
        .reshape(tok_rows, heads_total * HD)
    )
    key_rot = (
        jnp.repeat(apply_rope(key_pre, cosine_table, sine_table), copies, axis=1)
        .astype(jnp.bfloat16)
        .reshape(tok_rows, kv_total * copies * HD)
    )
    value_rep = (
        jnp.repeat(value_pre, copies, axis=1)
        .astype(jnp.bfloat16)
        .reshape(tok_rows, kv_total * copies * HD)
    )
    query_heads, key_heads, value_heads = (
        lax.all_to_all(query_rot, "sp", split_axis=1, concat_axis=0, tiled=True),
        lax.all_to_all(key_rot, "sp", split_axis=1, concat_axis=0, tiled=True),
        lax.all_to_all(value_rep, "sp", split_axis=1, concat_axis=0, tiled=True),
    )
    attn_heads, log_sums = attend(query_heads, key_heads, value_heads, documents, score_scale)
    attn_tokens = lax.all_to_all(attn_heads, "sp", split_axis=0, concat_axis=1, tiled=True)
    hidden_one = inputs + jnp.dot(attn_tokens, full_out, preferred_element_type=jnp.float32)
    inverse_two = lax.rsqrt(jnp.mean(hidden_one * hidden_one, axis=1, keepdims=True) + EPS)
    normed_two = hidden_one * inverse_two
    gain_two = full_gain_mlp.astype(jnp.float32)
    act_two = (normed_two * gain_two).astype(jnp.bfloat16)

    def gather_rows(values):
        return lax.all_gather(values, "sp", axis=0, tiled=True)

    def summed_rows(term_rows):
        return lax.psum_scatter(
            term_rows(jnp.int32(0), lax.axis_size("sp") * tok_rows).astype(jnp.bfloat16),
            "sp",
            scatter_dimension=0,
            tiled=True,
        ).astype(jnp.float32)

    act_all = gather_rows(act_two)
    gate_value = jnp.dot(act_all, w_gate, preferred_element_type=jnp.float32)
    up_value = jnp.dot(act_all, w_up, preferred_element_type=jnp.float32)
    sigmoid_gate = jax.nn.sigmoid(gate_value)
    silu_gate = gate_value * sigmoid_gate
    hidden_all = (silu_gate * up_value).astype(jnp.bfloat16)

    def down_terms(first_row, row_count):
        return jnp.dot(hidden_all, w_down, preferred_element_type=jnp.float32)

    mlp_out = summed_rows(down_terms)
    cotangent_all = gather_rows(cotangent)
    grad_w_down = contract(hidden_all, cotangent_all, 0, 0)
    hidden_back = contract(cotangent_all, w_down, 1, 1)
    gate_back = (
        hidden_back * up_value * sigmoid_gate * (1.0 + gate_value * (1.0 - sigmoid_gate))
    ).astype(jnp.bfloat16)
    up_back = (hidden_back * silu_gate).astype(jnp.bfloat16)
    grad_w_gate = contract(act_all, gate_back, 0, 0)
    grad_w_up = contract(act_all, up_back, 0, 0)

    def input_terms(first_row, row_count):
        return contract(gate_back, w_gate, 1, 1) + contract(up_back, w_up, 1, 1)

    act_two_back = summed_rows(input_terms)
    layer_out = (hidden_one + mlp_out).astype(jnp.bfloat16)
    normed_back_two = act_two_back * gain_two
    grad_gain_mlp = jnp.sum(act_two_back * normed_two, axis=0)
    hidden_one_back = cotangent.astype(jnp.float32) + inverse_two * (
        normed_back_two - normed_two * jnp.mean(normed_back_two * normed_two, axis=1, keepdims=True)
    )
    branch_back = hidden_one_back.astype(jnp.bfloat16)
    attn_tokens_back = contract(branch_back, full_out, 1, 1).astype(jnp.bfloat16)
    attn_heads_back = lax.all_to_all(
        attn_tokens_back, "sp", split_axis=1, concat_axis=0, tiled=True
    )
    query_back, key_back, value_back = attend_back(
        query_heads, key_heads, value_heads, attn_heads_back, log_sums, documents, score_scale
    )
    query_rot_back, key_rot_back, value_rep_back = (
        lax.all_to_all(query_back, "sp", split_axis=0, concat_axis=1, tiled=True),
        lax.all_to_all(key_back, "sp", split_axis=0, concat_axis=1, tiled=True),
        lax.all_to_all(value_back, "sp", split_axis=0, concat_axis=1, tiled=True),
    )
    query_pre_back = (
        rope_back(
            query_rot_back.astype(jnp.float32).reshape(tok_rows, heads_total, HD),
            cosine_table,
            sine_table,
        )
        .astype(jnp.bfloat16)
        .reshape(tok_rows, heads_total * HD)
    )
    key_summed = (
        key_rot_back.astype(jnp.float32).reshape(tok_rows, kv_total, copies, HD).sum(axis=2)
    )
    key_pre_back = (
        rope_back(key_summed, cosine_table, sine_table)
        .astype(jnp.bfloat16)
        .reshape(tok_rows, kv_total * HD)
    )
    value_pre_back = (
        value_rep_back.astype(jnp.float32)
        .reshape(tok_rows, kv_total, copies, HD)
        .sum(axis=2)
        .astype(jnp.bfloat16)
        .reshape(tok_rows, kv_total * HD)
    )
    act_one_back = (
        contract(query_pre_back, full_query, 1, 1)
        + contract(key_pre_back, full_key, 1, 1)
        + contract(value_pre_back, full_value, 1, 1)
    )
    normed_back_one = act_one_back * gain_one
    grad_gain_attn = jnp.sum(act_one_back * normed_one, axis=0)
    grad_tokens = hidden_one_back + inverse_one * (
        normed_back_one - normed_one * jnp.mean(normed_back_one * normed_one, axis=1, keepdims=True)
    )
    grad_w_out = contract(attn_tokens, branch_back, 0, 0)
    grad_w_query = contract(act_one, query_pre_back, 0, 0)
    grad_w_key = contract(act_one, key_pre_back, 0, 0)
    grad_w_value = contract(act_one, value_pre_back, 0, 0)
    part_query, part_key, part_value, part_out, part_gain_attn, part_gain_mlp = (
        lax.psum_scatter(
            grad_w_query.astype(jnp.bfloat16), "sp", scatter_dimension=0, tiled=True
        ).astype(jnp.float32),
        lax.psum_scatter(
            grad_w_key.astype(jnp.bfloat16), "sp", scatter_dimension=0, tiled=True
        ).astype(jnp.float32),
        lax.psum_scatter(
            grad_w_value.astype(jnp.bfloat16), "sp", scatter_dimension=0, tiled=True
        ).astype(jnp.float32),
        lax.psum_scatter(
            grad_w_out.astype(jnp.bfloat16), "sp", scatter_dimension=0, tiled=True
        ).astype(jnp.float32),
        lax.psum_scatter(
            grad_gain_attn.astype(jnp.bfloat16), "sp", scatter_dimension=0, tiled=True
        ).astype(jnp.float32),
        lax.psum_scatter(
            grad_gain_mlp.astype(jnp.bfloat16), "sp", scatter_dimension=0, tiled=True
        ).astype(jnp.float32),
    )
    summed = (
        lax.psum(part_query.astype(jnp.bfloat16), "dp").astype(jnp.float32),
        lax.psum(part_key.astype(jnp.bfloat16), "dp").astype(jnp.float32),
        lax.psum(part_value.astype(jnp.bfloat16), "dp").astype(jnp.float32),
        lax.psum(part_out.astype(jnp.bfloat16), "dp").astype(jnp.float32),
        lax.psum(part_gain_attn.astype(jnp.bfloat16), "dp").astype(jnp.float32),
        lax.psum(part_gain_mlp.astype(jnp.bfloat16), "dp").astype(jnp.float32),
        lax.psum(grad_w_gate.astype(jnp.bfloat16), "dp").astype(jnp.float32),
        lax.psum(grad_w_up.astype(jnp.bfloat16), "dp").astype(jnp.float32),
        lax.psum(grad_w_down.astype(jnp.bfloat16), "dp").astype(jnp.float32),
    )
    return (
        layer_out,
        grad_tokens,
        summed[0],
        summed[1],
        summed[2],
        summed[3],
        summed[4],
        summed[5],
        summed[6],
        summed[7],
        summed[8],
    )


def solution(mesh):
    placed = (
        P(("dp", "sp"), None),
        P("dp", None),
        P("sp", None),
        P("sp", None),
        P("sp", None),
        P("sp", None),
        P("sp"),
        P("sp"),
        P(None, "sp"),
        P(None, "sp"),
        P("sp", None),
        P(("dp", "sp"), None),
    )
    return jax.shard_map(
        on_device,
        mesh=mesh,
        in_specs=placed,
        out_specs=(
            P(("dp", "sp"), None),
            P(("dp", "sp"), None),
            P("sp", None),
            P("sp", None),
            P("sp", None),
            P("sp", None),
            P("sp"),
            P("sp"),
            P(None, "sp"),
            P(None, "sp"),
            P("sp", None),
        ),
        check_vma=False,
    )
```

profile of v0, /device:TPU:0, one launch (start us, length us, event | category | flops | bytes accessed | tf_op | source)
XLA Modules:
  0.0 1266.3 jit_solution(5629695011541414640)
XLA Ops:
  10.7 10.3 all-gather
  24.8 15.8 %all-gather.11.cloned.1.call-done = bf16[2048,512]{1,0:T(8,128)(2,1)} async-done(((bf16[256,512]{1,0:T(8,128)(2,1)}), bf16[2048,512]{1,0:T(8,128)(2,1)}) %all-gather.11.cloned.1.call-update) | async-done | bytes 2097168 | tf_op jit(solution)/shard_map/all_gather | solution.py:279
  47.2 23.2 %all-gather.13.cloned.1.call-done = bf16[2048,512]{1,0:T(8,128)(2,1)} async-done(((bf16[256,512]{1,0:T(8,128)(2,1)}), bf16[2048,512]{1,0:T(8,128)(2,1)}) %all-gather.13.cloned.1.call-update) | async-done | bytes 2097168 | tf_op jit(solution)/shard_map/all_gather | solution.py:280
  73.2 53.4 %all-gather.9.cloned.1.call-done = bf16[2048,2048]{1,0:T(8,128)(2,1)} async-done(((bf16[256,2048]{1,0:T(8,128)(2,1)}), bf16[2048,2048]{1,0:T(8,128)(2,1)}) %all-gather.9.cloned.1.call-update) | async-done | bytes 8388624 | tf_op jit(solution)/shard_map/all_gather | solution.py:278
  151.9 10.8 all-to-all-done
  163.7 15.2 %while.140 = (s32[]{:T(128)}, bf16[1024,256]{1,0:T(8,128)(2,1)}, f32[4,1024]{1,0:T(4,128)S(1)}, bf16[1024,256]{0,1:T(8,128)(2,1)S(1)}, s32[1024]{0:T(1024)S(1)},...) while((s32[]{:T(128)}, bf16[1024,256]{1,0:T(8,128)(2,1)}, ...), condition=%wide.region_11.12_spmd, body=%wide.region_4.11_spmd.sunk | while | flops 416030720 | bytes 14947181 | solution.py:159
  182.4 12.7 all-gather.1
  202.2 35.1 %all-gather.17.cloned.1.call-done = bf16[1024,2048]{1,0:T(8,128)(2,1)} async-done(((bf16[128,2048]{1,0:T(8,128)(2,1)}), bf16[1024,2048]{1,0:T(8,128)(2,1)}) %all-gather.17.cloned.1.call-update) | async-done | bytes 4194320 | tf_op jit(solution)/shard_map/all_gather | solution.py:336
  237.3 10.1 fusion.86
  253.4 22.4 %all-gather.19.cloned.1.call-done = bf16[1024,2048]{1,0:T(8,128)(2,1)} async-done(((bf16[128,2048]{1,0:T(8,128)(2,1)}), bf16[1024,2048]{1,0:T(8,128)(2,1)}) %all-gather.19.cloned.1.call-update) | async-done | bytes 4194320 | tf_op jit(solution)/shard_map/all_gather | solution.py:336
  275.8 13.3 %multiply_convert_fusion = (bf16[1024,1024]{1,0:T(8,128)(2,1)S(1)}, bf16[1024,1024]{1,0:T(8,128)(2,1)S(1)}, bf16[1024,1024]{1,0:T(8,128)(2,1)}) fusion(f32[1024,1024]{1,0:T(8,128)} %fusion.86, f32[1024,1024]{1,0:T(8,128)} %fusion.87, bf16[1024,2048]{1,0:T(8,128)(2,1)} %all-gather.19.cloned.1.call-done, bf16[1024,2048]{1,0:T(8,128)(2,1)} %param.34), kind=kOutput, calls=%fused_computation.83 | convolution fusion | flops 4310695936 | bytes 23068672 | tf_op jit(solution)/shard_map/dot_general | solution.py:61
  314.2 41.7 %reduce-scatter.9.cloned.1.call-done = bf16[128,2048]{1,0:T(8,128)(2,1)} async-done(((bf16[1024,2048]{1,0:T(8,128)(2,1)}), bf16[128,2048]{1,0:T(8,128)(2,1)}) %reduce-scatter.9.cloned.1.call-update) | async-done | bytes 524304 | tf_op jit(solution)/shard_map/reduce_scatter | solution.py:339
  357.9 53.6 %reduce-scatter.7.cloned.1.call-done = bf16[128,2048]{1,0:T(8,128)(2,1)} async-done(((bf16[1024,2048]{1,0:T(8,128)(2,1)}), bf16[128,2048]{1,0:T(8,128)(2,1)}) %reduce-scatter.7.cloned.1.call-update) | async-done | bytes 524304 | tf_op jit(solution)/shard_map/reduce_scatter | solution.py:339
  425.0 9.6 all-to-all-done.4
  436.2 30.8 %while.143 = (s32[]{:T(128)}, bf16[1024,256]{1,0:T(8,128)(2,1)}, f32[1024,1,64]{0,2,1:T(8,128)S(1)}, f32[1024,1,64]{0,2,1:T(8,128)}, bf16[1024,256]{0,1:T(8,128)...) while((s32[]{:T(128)}, bf16[1024,256]{1,0:T(8,128)(2,1)}, ...), condition=%wide.region_23.24_spmd, body=%wide.region_16.23_spmd.sunk | while | flops 957515776 | bytes 36893668 | solution.py:251
  452.6 13.5 %while.147 = (s32[]{:T(128)}, f32[512,4,64]{0,2,1:T(8,128)S(1)}, f32[1024,1,64]{0,2,1:T(8,128)S(1)}, f32[1024,1,64]{0,2,1:T(8,128)}, s32[]{:T(128)}, /*index=5*/...) while((s32[]{:T(128)}, f32[512,4,64]{0,2,1:T(8,128)S(1)}, ...), condition=%wide.region_22.22_spmd.clone, body=%wide.region_20.21_spmd.clone.sunk | while | flops 682918912 | bytes 23044332 | solution.py:232
  495.6 17.3 %all_to_all.133 = bf16[8,128,256]{2,1,0:T(8,128)(2,1)S(1)} all-to-all(bf16[8,128,256]{2,1,0:T(8,128)(2,1)S(1)} %bitcast.272), channel_id=1, replica_groups=mesh['dp'=4,'sp'=8] {'sp'}, dimensions={0} | all-to-all | bytes 1048576 | tf_op jit(solution)/shard_map/all_to_all | solution.py:386
  521.8 9.7 convolution_convert_fusion.3
  544.0 25.1 %reduce-scatter.15.cloned.1.call-done = bf16[256,512]{1,0:T(8,128)(2,1)} async-done(((bf16[2048,512]{1,0:T(8,128)(2,1)}), bf16[256,512]{1,0:T(8,128)(2,1)}) %reduce-scatter.15.cloned.1.call-update) | async-done | bytes 262160 | tf_op jit(solution)/shard_map/reduce_scatter | solution.py:435
  569.1 75.3 %reduce-scatter.17.cloned.1.call-done = bf16[256,2048]{1,0:T(8,128)(2,1)} async-done(((bf16[2048,2048]{1,0:T(8,128)(2,1)}), bf16[256,2048]{1,0:T(8,128)(2,1)}) %reduce-scatter.17.cloned.1.call-update) | async-done | bytes 1048592 | tf_op jit(solution)/shard_map/reduce_scatter | solution.py:438
  644.5 75.6 %reduce-scatter.11.cloned.1.call-done = bf16[256,2048]{1,0:T(8,128)(2,1)} async-done(((bf16[2048,2048]{1,0:T(8,128)(2,1)}), bf16[256,2048]{1,0:T(8,128)(2,1)}) %reduce-scatter.11.cloned.1.call-update) | async-done | bytes 1048592 | tf_op jit(solution)/shard_map/reduce_scatter | solution.py:429
  731.4 13.4 %all-reduce.2 = (bf16[2048]{0:T(1024)(128)(2,1)S(1)}, bf16[2048]{0:T(1024)(128)(2,1)S(1)}) all-reduce(bf16[2048]{0:T(1024)(128)(2,1)S(1)} %get-tuple-element.763, bf16[2048]{0:T(1024)(128)(2,1)S(1)} %copy-done.24), channel_id=8, replica_groups=mesh['dp'=4,'sp'=8] {'sp'}, use_global_device_ids=true, to_apply=%region_34.35.clone | all-reduce | flops 4096 | bytes 16384
  745.0 12.0 all-reduce.3
  759.5 479.5 %all-reduce.7.cloned.1.call-done = (bf16[256,2048]{1,0:T(8,128)(2,1)}, bf16[256,512]{1,0:T(8,128)(2,1)}, bf16[256,512]{1,0:T(8,128)(2,1)}, bf16[256,2048]{1,0:T(...) async-done(((bf16[256,2048]{1,0:T(8,128)(2,1)}, bf16[256,512]{1,0:T(8,128)(2,1)}, bf16[256,512]{1,0:T(8,128)(2,1)}, ...) | async-done | bytes 15204368 | tf_op jit(solution)/shard_map/psum | solution.py:449
  (343 shorter events, 257.5 us)
Async XLA Ops:
  7.2 33.4 %all-gather.11.cloned.1.call-start = ((), (), s32[]{:S(2)}) async-start(), calls=%async_computation.15 | async-start | bytes 2359296 | tf_op jit(solution)/shard_map/all_gather | solution.py:279
  7.9 62.4 %all-gather.13.cloned.1.call-start = ((), (), s32[]{:S(2)}) async-start(), calls=%async_computation.16 | async-start | bytes 2359296 | tf_op jit(solution)/shard_map/all_gather | solution.py:280
  8.7 118.0 %all-gather.9.cloned.1.call-start = ((), (), s32[]{:S(2)}) async-start(), calls=%async_computation.14 | async-start | bytes 9437184 | tf_op jit(solution)/shard_map/all_gather | solution.py:278
  9.4 186.0 %all-gather.15.cloned.1.call-start = ((), (), s32[]{:S(2)}) async-start(), calls=%async_computation.17 | async-start | bytes 9437184 | tf_op jit(solution)/shard_map/all_gather | solution.py:281
  21.0 105.7 %copy-start.12 = (f32[8,1,256]{2,1,0:T(1,128)}, f32[8,1,256]{2,1,0:T(1,128)S(1)}, u32[]{:S(2)}) copy-start(f32[8,1,256]{2,1,0:T(1,128)S(1)} %convert_element_type.279) | copy-start | bytes 24580
  22.3 104.4 %copy-start.22 = (f32[128]{0:T(128)}, f32[128]{0:T(128)S(1)}, u32[]{:S(2)}) copy-start(f32[128]{0:T(128)S(1)} %add_rsqrt_fusion.1) | copy-start | bytes 1540
  24.0 110.0 %copy-start.16 = (f32[128,64]{0,1:T(8,128)}, f32[128,64]{0,1:T(8,128)S(1)}, u32[]{:S(2)}) copy-start(f32[128,64]{0,1:T(8,128)S(1)} %pad_maximum_fusion.1) | copy-start | bytes 98308
  43.8 93.9 %all-to-all-start.1 = ((bf16[128,8,64]{0,2,1:T(8,128)(2,1)}), bf16[128,8,64]{0,2,1:T(8,128)(2,1)S(1)}, u32[]{:S(2)}, u32[]{:S(2)}) async-start(bf16[128,8,64]{0,2,1:T(8,128)(2,1)} %bitcast.18), calls=%async_computation.1 | async-start | bytes 262144 | tf_op jit(solution)/shard_map/all_to_all | solution.py:324
  137.7 10.6 all-to-all-start.2
  148.3 14.3 %all-to-all-start = ((bf16[128,8,256]{2,0,1:T(8,128)(2,1)}), bf16[128,8,256]{2,0,1:T(8,128)(2,1)S(1)}, u32[]{:S(2)}, u32[]{:S(2)}) async-start(bf16[128,8,256]{2,0,1:T(8,128)(2,1)} %bitcast.201), calls=%async_computation | async-start | bytes 1048576 | tf_op jit(solution)/shard_map/all_to_all | solution.py:323
  178.9 16.2 %all-to-all-start.3 = ((bf16[8,128,256]{2,1,0:T(8,128)(2,1)}), bf16[8,128,256]{2,1,0:T(8,128)(2,1)S(1)}, u32[]{:S(2)}, u32[]{:S(2)}) async-start(bf16[8,128,256]{2,1,0:T(8,128)(2,1)} %bitcast.22), calls=%async_computation.3 | async-start | bytes 1048576 | tf_op jit(solution)/shard_map/all_to_all | solution.py:328
  182.4 54.9 %all-gather.17.cloned.1.call-start = ((), (), s32[]{:S(2)}) async-start(), calls=%async_computation.18 | async-start | bytes 4718592 | tf_op jit(solution)/shard_map/all_gather | solution.py:336
  201.4 74.4 %all-gather.19.cloned.1.call-start = ((), (), s32[]{:S(2)}) async-start(), calls=%async_computation.20 | async-start | bytes 4718592 | tf_op jit(solution)/shard_map/all_gather | solution.py:336
  201.9 153.9 %reduce-scatter.9.cloned.1.call-start = ((), (), s32[]{:S(2)}) async-start(), calls=%async_computation.21 | async-start | bytes 4718592 | tf_op jit(solution)/shard_map/reduce_scatter | solution.py:339
  304.4 107.2 %reduce-scatter.7.cloned.1.call-start = ((), (), s32[]{:S(2)}) async-start(), calls=%async_computation.19 | async-start | bytes 4718592 | tf_op jit(solution)/shard_map/reduce_scatter | solution.py:339
  314.1 97.4 %copy-start.9 = (bf16[128,2048]{1,0:T(8,128)(2,1)S(1)}, bf16[128,2048]{1,0:T(8,128)(2,1)}, u32[]{:S(2)}) copy-start(bf16[128,2048]{1,0:T(8,128)(2,1)} %param.35) | copy-start | bytes 1572868
  421.4 13.2 %all-to-all-start.4 = ((bf16[128,8,256]{2,0,1:T(8,128)(2,1)}), bf16[128,8,256]{2,0,1:T(8,128)(2,1)S(1)}, u32[]{:S(2)}, u32[]{:S(2)}) async-start(bf16[128,8,256]{2,0,1:T(8,128)(2,1)} %bitcast.200), calls=%async_computation.6 | async-start | bytes 1048576 | tf_op jit(solution)/shard_map/all_to_all | solution.py:379
  424.9 119.1 %reduce-scatter.13.cloned.1.call-start = ((), (), s32[]{:S(2)}) async-start(), calls=%async_computation.23 | async-start | bytes 2359296 | tf_op jit(solution)/shard_map/reduce_scatter | solution.py:432
  436.2 39.9 %copy-start.13 = (f32[8,1,256]{2,1,0:T(1,128)S(1)}, f32[8,1,256]{2,1,0:T(1,128)}, u32[]{:S(2)}) copy-start(f32[8,1,256]{2,1,0:T(1,128)} %copy-done.12) | copy-start | bytes 24580
  436.2 39.9 %copy-start.23 = (f32[128]{0:T(128)S(1)}, f32[128]{0:T(128)}, u32[]{:S(2)}) copy-start(f32[128]{0:T(128)} %copy-done.22) | copy-start | bytes 1540
  478.3 90.8 %reduce-scatter.15.cloned.1.call-start = ((), (), s32[]{:S(2)}) async-start(), calls=%async_computation.24 | async-start | bytes 2359296 | tf_op jit(solution)/shard_map/reduce_scatter | solution.py:435
  488.7 155.7 %reduce-scatter.17.cloned.1.call-start = ((), (), s32[]{:S(2)}) async-start(), calls=%async_computation.25 | async-start | bytes 9437184 | tf_op jit(solution)/shard_map/reduce_scatter | solution.py:438
  494.6 225.5 %reduce-scatter.11.cloned.1.call-start = ((), (), s32[]{:S(2)}) async-start(), calls=%async_computation.22 | async-start | bytes 9437184 | tf_op jit(solution)/shard_map/reduce_scatter | solution.py:429
  521.7 717.3 %all-reduce.7.cloned.1.call-start = ((), (), s32[]{:S(2)}) async-start(), calls=%async_computation.26 | async-start | bytes 30408704 | tf_op jit(solution)/shard_map/psum | solution.py:449
  (31 other events, 351.4 us)
Sparse Core Ops, SparseCore 0:
  9.9 30.5 all-gather.10
  42.4 27.8 all-gather.12
  72.2 54.3 all-gather.8
  128.4 57.1 all-gather.14
  201.5 35.7 all-gather.16
  239.1 36.7 all-gather.18
  304.5 51.3 reduce-scatter.8
  360.1 51.3 reduce-scatter.6
  478.4 45.8 reduce-scatter.12
  527.8 41.2 reduce-scatter.14
  573.2 71.2 reduce-scatter.16
  648.8 71.2 reduce-scatter.10
  724.1 514.8 all-reduce.6
where the time goes:
time: 1280 us; the launch traced here: 1270 us
  waiting for transfers between devices  929 us (73%)
  matrix products  154 us (12%)
  blocking collectives  81.6 us (6%)
  other arithmetic  44.4 us (3%)
  local copies, waits for them, and re-layouts  22.4 us (2%)
  starting transfers between devices  18.3 us (1%)
  between operations  15.4 us (1%)
    psum x1, waiting for transfers between devices, on_device(): lax.psum(part_query.astype(jnp.bfloat16), 'dp').astype(jnp.float32)  480 us
    reduce_scatter x2, waiting for transfers between devices, summed_rows(): lax.psum_scatter(term_rows(jnp.int32(0), lax.axis_size('sp') * tok_rows)....  95.3 us
    dot_general x14, matrix products, contract(): lax.dot_general(left, right, (((left_dim,), (right_dim,)), ((), ())), pre...  81.6 us
    reduce_scatter x1, waiting for transfers between devices, on_device(): lax.psum_scatter(grad_w_query.astype(jnp.bfloat16), 'sp', scatter_dimensi...  75.6 us
    reduce_scatter x1, waiting for transfers between devices, on_device(): lax.psum_scatter(grad_w_out.astype(jnp.bfloat16), 'sp', scatter_dimension...  75.3 us
    all_gather x2, waiting for transfers between devices, gather_rows(): return lax.all_gather(values, 'sp', axis=0, tiled=True)  57.5 us
    all_gather x1, waiting for transfers between devices, on_device(): lax.all_gather(w_query, 'sp', axis=0, tiled=True)  53.4 us
  transfers between devices with their start and end apart: 18, of which 14 were waited for; matrix products, arithmetic and copies ran while one was open for 9% of the time, Pallas kernels for 0%

commit v1 on v0

--- a/solution.py
+++ b/solution.py
@@ -27,7 +27,9 @@
 
 
 def doc_layout(lengths, first_row, row_total):
-    ends_at = jnp.cumsum(lengths)
+    count = lengths.shape[0]
+    upto = jnp.arange(count)[None, :] <= jnp.arange(count)[:, None]
+    ends_at = jnp.sum(jnp.where(upto, lengths[None, :], 0), axis=1)
     starts_at = ends_at - lengths
     places = first_row + jnp.arange(row_total, dtype=jnp.int32)
     documents = jnp.sum((places[:, None] >= ends_at[None, :]).astype(jnp.int32), axis=1)
@@ -254,6 +256,136 @@
         key_grads.reshape(total_rows, local_kv * HD).astype(jnp.bfloat16),
         value_grads.reshape(total_rows, local_kv * HD).astype(jnp.bfloat16),
     )
+
+
+def swap(values, distance, axis):
+    size = lax.axis_size(axis)
+    return lax.ppermute(values, axis, [(i, i ^ distance) for i in range(size)])
+
+
+def block_order(shards):
+    return list(range(0, shards, 2)) + list(range(1, shards, 2))
+
+
+def gather_rel(values):
+    shards = lax.axis_size("sp")
+    if shards == 8:
+        half = values.shape[0] // 2
+        near = swap(values, 2, "sp")
+        next_row = swap(values, 4, "sp")
+        far = jnp.concatenate(
+            [swap(near[:half], 4, "sp"), swap(next_row[half:], 2, "sp")], axis=0
+        )
+        evens = [values, near, next_row, far]
+    else:
+        evens = [values]
+        distance = 2
+        while distance < shards:
+            evens = evens + [swap(block, distance, "sp") for block in evens]
+            distance *= 2
+    return evens + [swap(block, 1, "sp") for block in evens]
+
+
+def scatter_rel(even_terms, odd_terms):
+    shards = lax.axis_size("sp")
+    rows = even_terms.shape[0] // (shards // 2)
+    width = even_terms.shape[1]
+    got = swap(odd_terms.astype(jnp.bfloat16), 1, "sp")
+    sums = (even_terms + got.astype(jnp.float32)).reshape(shards // 2, rows, width)
+    if shards == 8:
+        half = rows // 2
+        far = sums[3].astype(jnp.bfloat16)
+        to_next = swap(far[:half], 2, "sp").astype(jnp.float32)
+        to_near = swap(far[half:], 4, "sp").astype(jnp.float32)
+        near = jnp.concatenate([sums[1][:half], sums[1][half:] + to_near], axis=0)
+        next_row = jnp.concatenate([sums[2][:half] + to_next, sums[2][half:]], axis=0)
+        return (
+            sums[0]
+            + swap(near.astype(jnp.bfloat16), 2, "sp").astype(jnp.float32)
+            + swap(next_row.astype(jnp.bfloat16), 4, "sp").astype(jnp.float32)
+        )
+    distance = shards // 2
+    while distance > 1:
+        kept = distance // 2
+        sums = sums[:kept] + swap(sums[kept:].astype(jnp.bfloat16), distance, "sp").astype(
+            jnp.float32
+        )
+        distance //= 2
+    return sums[0]
+
+
+def reorder(values, seq_rank):
+    shards = lax.axis_size("sp")
+    order = block_order(shards)
+    rows = values.shape[0] // shards
+    return jnp.concatenate(
+        [
+            lax.dynamic_slice_in_dim(values, (seq_rank ^ distance) * rows, rows, 0)
+            for distance in order
+        ],
+        axis=0,
+    )
+
+
+def to_token_order(values, seq_rank):
+    shards = lax.axis_size("sp")
+    order = block_order(shards)
+    place = jnp.asarray([order.index(k) for k in range(shards)], jnp.int32)
+    rows = values.shape[0] // shards
+    return jnp.concatenate(
+        [
+            lax.dynamic_slice_in_dim(values, place[seq_rank ^ index] * rows, rows, 0)
+            for index in range(shards)
+        ],
+        axis=0,
+    )
+
+
+def dp_scatter(terms):
+    groups = lax.axis_size("dp")
+    rank = lax.axis_index("dp")
+    total = lax.dynamic_index_in_dim(terms, rank, 0, keepdims=False)
+    for distance in range(1, groups):
+        piece = lax.dynamic_index_in_dim(terms, rank ^ distance, 0, keepdims=False)
+        total = total + swap(piece.astype(jnp.bfloat16), distance, "dp").astype(jnp.float32)
+    return total
+
+
+def dp_gather(piece):
+    groups = lax.axis_size("dp")
+    rank = lax.axis_index("dp")
+    whole = jnp.zeros((groups,) + piece.shape, piece.dtype)
+    for distance in range(groups):
+        block = piece if distance == 0 else swap(piece, distance, "dp")
+        whole = lax.dynamic_update_index_in_dim(whole, block, rank ^ distance, 0)
+    return whole
+
+
+def sum_all(values):
+    for axis in ("sp", "dp"):
+        distance = 1
+        while distance < lax.axis_size(axis):
+            values = values + swap(values, distance, axis)
+            distance *= 2
+    return values
+
+
+def silu_parts(gate_value):
+    sigmoid_gate = jax.nn.sigmoid(gate_value)
+    return sigmoid_gate, gate_value * sigmoid_gate
+
+
+def feed_forward(act_rows, cot_rows, w_gate, w_up, w_down):
+    gate_value = jnp.dot(act_rows, w_gate, preferred_element_type=jnp.float32)
+    up_value = jnp.dot(act_rows, w_up, preferred_element_type=jnp.float32)
+    hidden_back = contract(cot_rows, w_down, 1, 1)
+    sigmoid_gate, silu_gate = silu_parts(gate_value)
+    hidden = (silu_gate * up_value).astype(jnp.bfloat16)
+    gate_back = (
+        hidden_back * up_value * sigmoid_gate * (1.0 + gate_value * (1.0 - sigmoid_gate))
+    ).astype(jnp.bfloat16)
+    up_back = (hidden_back * silu_gate).astype(jnp.bfloat16)
+    return hidden, gate_back, up_back
 
 
 def on_device(
@@ -271,203 +403,198 @@
     cotangent,
 ):
     shards = lax.axis_size("sp")
+    groups = lax.axis_size("dp")
     seq_rank = lax.axis_index("sp")
-    tok_rows = tokens.shape[0]
+    tok_rows, width = tokens.shape
     group_rows = tok_rows * shards
-    full_query, full_key, full_value, full_out, full_gain_attn, full_gain_mlp = (
-        lax.all_gather(w_query, "sp", axis=0, tiled=True),
-        lax.all_gather(w_key, "sp", axis=0, tiled=True),
-        lax.all_gather(w_value, "sp", axis=0, tiled=True),
-        lax.all_gather(w_out, "sp", axis=0, tiled=True),
-        lax.all_gather(gain_attn, "sp", axis=0, tiled=True),
-        lax.all_gather(gain_mlp, "sp", axis=0, tiled=True),
-    )
-    heads_total = full_query.shape[1] // HD
-    kv_total = full_key.shape[1] // HD
+    heads_total = w_query.shape[1] // HD
+    kv_total = w_key.shape[1] // HD
     copies = max(1, shards // kv_total)
+    q_cols = heads_total // shards * HD
+    kv_cols = kv_total * copies // shards * HD
+    part_rows = w_query.shape[0]
     score_scale = HD ** (-0.5)
     lengths = doc_lengths[0]
-    _, _, positions = doc_layout(lengths, seq_rank * tok_rows, tok_rows)
+    documents, _, positions = doc_layout(lengths, jnp.int32(0), group_rows)
     cosine_table, sine_table = rotation(positions, HD)
-    documents, _, _ = doc_layout(lengths, jnp.int32(0), group_rows)
+
+    token_rows = jnp.concatenate(gather_rel(tokens), axis=0)
+
+    def repeat_heads(weight):
+        rows = weight.shape[0]
+        return jnp.repeat(weight.reshape(rows, kv_total, 1, HD), copies, axis=2).reshape(
+            rows, shards, kv_cols
+        )
+
+    w_mixed = jnp.concatenate(
+        [
+            w_query.reshape(part_rows, shards, q_cols),
+            repeat_heads(w_key),
+            repeat_heads(w_value),
+        ],
+        axis=2,
+    )
+    w_local = lax.all_to_all(
+        jnp.transpose(w_mixed, (1, 0, 2)), "sp", split_axis=0, concat_axis=0, tiled=True
+    ).reshape(width, q_cols + 2 * kv_cols)
+    gains = lax.all_gather(jnp.stack([gain_attn, gain_mlp]), "sp", axis=1, tiled=True).astype(
+        jnp.float32
+    )
+    gain_one, gain_two = gains[0], gains[1]
+
+    def normed(values):
+        inverse = lax.rsqrt(jnp.mean(values * values, axis=1, keepdims=True) + EPS)
+        return inverse, values * inverse
+
     inputs = tokens.astype(jnp.float32)
-    inverse_one = lax.rsqrt(jnp.mean(inputs * inputs, axis=1, keepdims=True) + EPS)
-    normed_one = inputs * inverse_one
-    gain_one = full_gain_attn.astype(jnp.float32)
-    act_one = (normed_one * gain_one).astype(jnp.bfloat16)
-    query_pre = jnp.dot(act_one, full_query, preferred_element_type=jnp.float32).reshape(
-        tok_rows, heads_total, HD
-    )
-    key_pre = jnp.dot(act_one, full_key, preferred_element_type=jnp.float32).reshape(
-        tok_rows, kv_total, HD
-    )
-    value_pre = jnp.dot(act_one, full_value, preferred_element_type=jnp.float32).reshape(
-        tok_rows, kv_total, HD
-    )
-    query_rot = (
-        apply_rope(query_pre, cosine_table, sine_table)
+    inverse_one, normed_one = normed(inputs)
+    _, normed_rows = normed(token_rows.astype(jnp.float32))
+    act_one = (normed_rows * gain_one).astype(jnp.bfloat16)
+    mixed = to_token_order(
+        jnp.dot(act_one, w_local, preferred_element_type=jnp.float32), seq_rank
+    )
+    query_heads = (
+        apply_rope(mixed[:, :q_cols].reshape(group_rows, q_cols // HD, HD), cosine_table, sine_table)
         .astype(jnp.bfloat16)
-        .reshape(tok_rows, heads_total * HD)
-    )
-    key_rot = (
-        jnp.repeat(apply_rope(key_pre, cosine_table, sine_table), copies, axis=1)
+        .reshape(group_rows, q_cols)
+    )
+    key_heads = (
+        apply_rope(
+            mixed[:, q_cols : q_cols + kv_cols].reshape(group_rows, kv_cols // HD, HD),
+            cosine_table,
+            sine_table,
+        )
         .astype(jnp.bfloat16)
-        .reshape(tok_rows, kv_total * copies * HD)
-    )
-    value_rep = (
-        jnp.repeat(value_pre, copies, axis=1)
-        .astype(jnp.bfloat16)
-        .reshape(tok_rows, kv_total * copies * HD)
-    )
-    query_heads, key_heads, value_heads = (
-        lax.all_to_all(query_rot, "sp", split_axis=1, concat_axis=0, tiled=True),
-        lax.all_to_all(key_rot, "sp", split_axis=1, concat_axis=0, tiled=True),
-        lax.all_to_all(value_rep, "sp", split_axis=1, concat_axis=0, tiled=True),
-    )
+        .reshape(group_rows, kv_cols)
+    )
+    value_heads = mixed[:, q_cols + kv_cols :].astype(jnp.bfloat16)
     attn_heads, log_sums = attend(query_heads, key_heads, value_heads, documents, score_scale)
-    attn_tokens = lax.all_to_all(attn_heads, "sp", split_axis=0, concat_axis=1, tiled=True)
-    hidden_one = inputs + jnp.dot(attn_tokens, full_out, preferred_element_type=jnp.float32)
-    inverse_two = lax.rsqrt(jnp.mean(hidden_one * hidden_one, axis=1, keepdims=True) + EPS)
-    normed_two = hidden_one * inverse_two
-    gain_two = full_gain_mlp.astype(jnp.float32)
+    attn_rel = reorder(attn_heads, seq_rank)
+    half_rows = group_rows // 2
+
+    def product_terms(term):
+        odd = term(slice(half_rows, group_rows))
+        even = term(slice(0, half_rows))
+        return scatter_rel(even, odd)
+
+    hidden_one = inputs + product_terms(
+        lambda rows: jnp.dot(attn_rel[rows], w_out, preferred_element_type=jnp.float32)
+    )
+    inverse_two, normed_two = normed(hidden_one)
     act_two = (normed_two * gain_two).astype(jnp.bfloat16)
 
-    def gather_rows(values):
-        return lax.all_gather(values, "sp", axis=0, tiled=True)
-
-    def summed_rows(term_rows):
-        return lax.psum_scatter(
-            term_rows(jnp.int32(0), lax.axis_size("sp") * tok_rows).astype(jnp.bfloat16),
-            "sp",
-            scatter_dimension=0,
-            tiled=True,
-        ).astype(jnp.float32)
-
-    act_all = gather_rows(act_two)
-    gate_value = jnp.dot(act_all, w_gate, preferred_element_type=jnp.float32)
-    up_value = jnp.dot(act_all, w_up, preferred_element_type=jnp.float32)
-    sigmoid_gate = jax.nn.sigmoid(gate_value)
-    silu_gate = gate_value * sigmoid_gate
-    hidden_all = (silu_gate * up_value).astype(jnp.bfloat16)
-
-    def down_terms(first_row, row_count):
-        return jnp.dot(hidden_all, w_down, preferred_element_type=jnp.float32)
-
-    mlp_out = summed_rows(down_terms)
-    cotangent_all = gather_rows(cotangent)
-    grad_w_down = contract(hidden_all, cotangent_all, 0, 0)
-    hidden_back = contract(cotangent_all, w_down, 1, 1)
-    gate_back = (
-        hidden_back * up_value * sigmoid_gate * (1.0 + gate_value * (1.0 - sigmoid_gate))
-    ).astype(jnp.bfloat16)
-    up_back = (hidden_back * silu_gate).astype(jnp.bfloat16)
-    grad_w_gate = contract(act_all, gate_back, 0, 0)
-    grad_w_up = contract(act_all, up_back, 0, 0)
-
-    def input_terms(first_row, row_count):
-        return contract(gate_back, w_gate, 1, 1) + contract(up_back, w_up, 1, 1)
-
-    act_two_back = summed_rows(input_terms)
+    cot_blocks = gather_rel(cotangent)
+    cot_rows = jnp.concatenate(cot_blocks, axis=0)
+    act_rows = jnp.concatenate(gather_rel(act_two), axis=0)
+    hidden, gate_back, up_back = feed_forward(act_rows, cot_rows, w_gate, w_up, w_down)
+    act_two_back = product_terms(
+        lambda rows: contract(gate_back[rows], w_gate, 1, 1) + contract(up_back[rows], w_up, 1, 1)
+    )
+    mlp_out = product_terms(
+        lambda rows: jnp.dot(hidden[rows], w_down, preferred_element_type=jnp.float32)
+    )
     layer_out = (hidden_one + mlp_out).astype(jnp.bfloat16)
+    grad_down = contract(hidden, cot_rows, 0, 0)
+    grad_gate = contract(act_rows, gate_back, 0, 0)
+    grad_up = contract(act_rows, up_back, 0, 0)
+    if groups <= 4:
+        for distance in range(1, groups):
+            cot_other = jnp.concatenate(gather_rel(swap(cotangent, distance, "dp")), axis=0)
+            act_other = jnp.concatenate(gather_rel(swap(act_two, distance, "dp")), axis=0)
+            hidden_o, gate_o, up_o = feed_forward(act_other, cot_other, w_gate, w_up, w_down)
+            grad_down = grad_down + contract(hidden_o, cot_other, 0, 0)
+            grad_gate = grad_gate + contract(act_other, gate_o, 0, 0)
+            grad_up = grad_up + contract(act_other, up_o, 0, 0)
+    else:
+        grad_down, grad_gate, grad_up = (
+            lax.psum(grad.astype(jnp.bfloat16), "dp").astype(jnp.float32)
+            for grad in (grad_down, grad_gate, grad_up)
+        )
+
     normed_back_two = act_two_back * gain_two
-    grad_gain_mlp = jnp.sum(act_two_back * normed_two, axis=0)
+    gain_mlp_terms = jnp.sum(act_two_back * normed_two, axis=0)
     hidden_one_back = cotangent.astype(jnp.float32) + inverse_two * (
         normed_back_two - normed_two * jnp.mean(normed_back_two * normed_two, axis=1, keepdims=True)
     )
-    branch_back = hidden_one_back.astype(jnp.bfloat16)
-    attn_tokens_back = contract(branch_back, full_out, 1, 1).astype(jnp.bfloat16)
-    attn_heads_back = lax.all_to_all(
-        attn_tokens_back, "sp", split_axis=1, concat_axis=0, tiled=True
-    )
+    branch_rows = jnp.concatenate(gather_rel(hidden_one_back.astype(jnp.bfloat16)), axis=0)
+    heads_back = to_token_order(
+        contract(branch_rows, w_out, 1, 1).astype(jnp.bfloat16), seq_rank
+    )
+    grad_out_terms = contract(attn_rel, branch_rows, 0, 0)
+    grad_out = (
+        dp_gather(
+            dp_scatter(grad_out_terms.reshape(groups, -1, width)).astype(jnp.bfloat16)
+        )
+        .astype(jnp.float32)
+        .reshape(grad_out_terms.shape)
+    )
+
     query_back, key_back, value_back = attend_back(
-        query_heads, key_heads, value_heads, attn_heads_back, log_sums, documents, score_scale
-    )
-    query_rot_back, key_rot_back, value_rep_back = (
-        lax.all_to_all(query_back, "sp", split_axis=0, concat_axis=1, tiled=True),
-        lax.all_to_all(key_back, "sp", split_axis=0, concat_axis=1, tiled=True),
-        lax.all_to_all(value_back, "sp", split_axis=0, concat_axis=1, tiled=True),
-    )
-    query_pre_back = (
-        rope_back(
-            query_rot_back.astype(jnp.float32).reshape(tok_rows, heads_total, HD),
-            cosine_table,
-            sine_table,
-        )
-        .astype(jnp.bfloat16)
-        .reshape(tok_rows, heads_total * HD)
-    )
-    key_summed = (
-        key_rot_back.astype(jnp.float32).reshape(tok_rows, kv_total, copies, HD).sum(axis=2)
-    )
-    key_pre_back = (
-        rope_back(key_summed, cosine_table, sine_table)
-        .astype(jnp.bfloat16)
-        .reshape(tok_rows, kv_total * HD)
-    )
-    value_pre_back = (
-        value_rep_back.astype(jnp.float32)
-        .reshape(tok_rows, kv_total, copies, HD)
-        .sum(axis=2)
-        .astype(jnp.bfloat16)
-        .reshape(tok_rows, kv_total * HD)
-    )
-    act_one_back = (
-        contract(query_pre_back, full_query, 1, 1)
-        + contract(key_pre_back, full_key, 1, 1)
-        + contract(value_pre_back, full_value, 1, 1)
-    )
+        query_heads, key_heads, value_heads, heads_back, log_sums, documents, score_scale
+    )
+    mixed_back = reorder(
+        jnp.concatenate(
+            [
+                rope_back(
+                    query_back.astype(jnp.float32).reshape(group_rows, q_cols // HD, HD),
+                    cosine_table,
+                    sine_table,
+                )
+                .astype(jnp.bfloat16)
+                .reshape(group_rows, q_cols),
+                rope_back(
+                    key_back.astype(jnp.float32).reshape(group_rows, kv_cols // HD, HD),
+                    cosine_table,
+                    sine_table,
+                )
+                .astype(jnp.bfloat16)
+                .reshape(group_rows, kv_cols),
+                value_back,
+            ],
+            axis=1,
+        ),
+        seq_rank,
+    )
+    act_one_back = product_terms(lambda rows: contract(mixed_back[rows], w_local, 1, 1))
+    grad_mixed = contract(act_one, mixed_back, 0, 0)
+    strip = width // (shards * groups)
+    columns = grad_mixed.shape[1]
+    grad_strip = dp_scatter(
+        jnp.transpose(grad_mixed.reshape(shards, groups, strip, columns), (1, 0, 2, 3))
+    )
+    grad_strip = lax.all_to_all(
+        grad_strip.astype(jnp.bfloat16), "sp", split_axis=0, concat_axis=0, tiled=True
+    )
+    grad_parts = dp_gather(grad_strip).astype(jnp.float32)
+    grad_parts = jnp.transpose(grad_parts, (0, 2, 1, 3)).reshape(part_rows, shards, columns)
+    grad_query = grad_parts[:, :, :q_cols].reshape(part_rows, shards * q_cols)
+
+    def sum_copies(parts):
+        return parts.reshape(part_rows, kv_total, copies, HD).sum(axis=2).reshape(part_rows, -1)
+
+    grad_key = sum_copies(grad_parts[:, :, q_cols : q_cols + kv_cols])
+    grad_value = sum_copies(grad_parts[:, :, q_cols + kv_cols :])
+
     normed_back_one = act_one_back * gain_one
-    grad_gain_attn = jnp.sum(act_one_back * normed_one, axis=0)
+    gain_attn_terms = jnp.sum(act_one_back * normed_one, axis=0)
     grad_tokens = hidden_one_back + inverse_one * (
         normed_back_one - normed_one * jnp.mean(normed_back_one * normed_one, axis=1, keepdims=True)
     )
-    grad_w_out = contract(attn_tokens, branch_back, 0, 0)
-    grad_w_query = contract(act_one, query_pre_back, 0, 0)
-    grad_w_key = contract(act_one, key_pre_back, 0, 0)
-    grad_w_value = contract(act_one, value_pre_back, 0, 0)
-    part_query, part_key, part_value, part_out, part_gain_attn, part_gain_mlp = (
-        lax.psum_scatter(
-            grad_w_query.astype(jnp.bfloat16), "sp", scatter_dimension=0, tiled=True
-        ).astype(jnp.float32),
-        lax.psum_scatter(
-            grad_w_key.astype(jnp.bfloat16), "sp", scatter_dimension=0, tiled=True
-        ).astype(jnp.float32),
-        lax.psum_scatter(
-            grad_w_value.astype(jnp.bfloat16), "sp", scatter_dimension=0, tiled=True
-        ).astype(jnp.float32),
-        lax.psum_scatter(
-            grad_w_out.astype(jnp.bfloat16), "sp", scatter_dimension=0, tiled=True
-        ).astype(jnp.float32),
-        lax.psum_scatter(
-            grad_gain_attn.astype(jnp.bfloat16), "sp", scatter_dimension=0, tiled=True
-        ).astype(jnp.float32),
-        lax.psum_scatter(
-            grad_gain_mlp.astype(jnp.bfloat16), "sp", scatter_dimension=0, tiled=True
-        ).astype(jnp.float32),
-    )
-    summed = (
-        lax.psum(part_query.astype(jnp.bfloat16), "dp").astype(jnp.float32),
-        lax.psum(part_key.astype(jnp.bfloat16), "dp").astype(jnp.float32),
-        lax.psum(part_value.astype(jnp.bfloat16), "dp").astype(jnp.float32),
-        lax.psum(part_out.astype(jnp.bfloat16), "dp").astype(jnp.float32),
-        lax.psum(part_gain_attn.astype(jnp.bfloat16), "dp").astype(jnp.float32),
-        lax.psum(part_gain_mlp.astype(jnp.bfloat16), "dp").astype(jnp.float32),
-        lax.psum(grad_w_gate.astype(jnp.bfloat16), "dp").astype(jnp.float32),
-        lax.psum(grad_w_up.astype(jnp.bfloat16), "dp").astype(jnp.float32),
-        lax.psum(grad_w_down.astype(jnp.bfloat16), "dp").astype(jnp.float32),
+    grad_gains = lax.dynamic_slice_in_dim(
+        sum_all(jnp.stack([gain_attn_terms, gain_mlp_terms])), seq_rank * part_rows, part_rows, 1
     )
     return (
         layer_out,
         grad_tokens,
-        summed[0],
-        summed[1],
-        summed[2],
-        summed[3],
-        summed[4],
-        summed[5],
-        summed[6],
-        summed[7],
-        summed[8],
+        grad_query,
+        grad_key,
+        grad_value,
+        grad_out,
+        grad_gains[0],
+        grad_gains[1],
+        grad_gate,
+        grad_up,
+        grad_down,
     )
 
 

time: 1280 us -> 842 us (0.66)
  waiting for transfers between devices: 929 us -> 244 us
  matrix products: 154 us -> 302 us
  starting transfers between devices: 18.3 us -> 127 us
  local copies, waits for them, and re-layouts: 22.4 us -> 93.5 us
  blocking collectives: 81.6 us -> 22 us
    psum x1 -> x0, waiting for transfers between devices: 480 us -> none  [on_device(): lax.psum(part_query.astype(jnp.bfloat16), 'dp').astype(jnp.float32)]
    reduce_scatter x6 -> x0, waiting for transfers between devices: 271 us -> none  [the longest x2 95.3 us: summed_rows(): lax.psum_scatter(term_rows(jnp.int32(0), lax.axis_size('sp') * tok_rows)....]
    ppermute x0 -> x123, waiting for transfers between devices: none -> 244 us  [swap(): return lax.ppermute(values, axis, [(i, i ^ distance) for i in range(size)])]
    all_gather x6 -> x0, waiting for transfers between devices: 150 us -> none  [the longest x2 57.5 us: gather_rows(): return lax.all_gather(values, 'sp', axis=0, tiled=True)]
    dot_general x14 -> x25, matrix products: 81.6 us -> 215 us  [contract(): lax.dot_general(left, right, (((left_dim,), (right_dim,)), ((), ())), pre...]
    ppermute x0 -> x123, starting transfers between devices: none -> 119 us  [swap(): return lax.ppermute(values, axis, [(i, i ^ distance) for i in range(size)])]
    unnamed x81 -> x296, local copies, waits for them, and re-layouts: 4.37 us -> 57.2 us
    all_to_all x3 -> x0, blocking collectives: 33.3 us -> none  [the longest x1 17.3 us: on_device(): lax.all_to_all(query_back, 'sp', split_axis=0, concat_axis=1, tiled=True)]
  transfers between devices with their start and end apart: 18 -> 125, of which waited for: 14 -> 50; matrix products, arithmetic and copies ran while one was open for 9% -> 45% of each run, Pallas kernels for 0% -> 0%
where the time goes in v1:
time: 842 us; the launch traced here: 834 us
  matrix products  302 us (36%)
  waiting for transfers between devices  244 us (29%)
  starting transfers between devices  127 us (15%)
  local copies, waits for them, and re-layouts  93.5 us (11%)
  other arithmetic  35.5 us (4%)
  blocking collectives  22 us (3%)
  between operations  8.95 us (1%)
    ppermute x123, waiting for transfers between devices, swap(): return lax.ppermute(values, axis, [(i, i ^ distance) for i in range(size)])  244 us
    dot_general x25, matrix products, contract(): lax.dot_general(left, right, (((left_dim,), (right_dim,)), ((), ())), pre...  215 us
    ppermute x123, starting transfers between devices, swap(): return lax.ppermute(values, axis, [(i, i ^ distance) for i in range(size)])  119 us
    unnamed x296, local copies, waits for them, and re-layouts  57.2 us
    dot_general x4, matrix products, feed_forward(): up_value = jnp.dot(act_rows, w_up, preferred_element_type=jnp.float32)  23 us
    all_gather x1, blocking collectives, on_device(): lax.all_gather(jnp.stack([gain_attn, gain_mlp]), 'sp', axis=1, tiled=True)  22 us
    dot_general x4, matrix products, feed_forward(): gate_value = jnp.dot(act_rows, w_gate, preferred_element_type=jnp.float32)  21.3 us
  transfers between devices with their start and end apart: 125, of which 50 were waited for; matrix products, arithmetic and copies ran while one was open for 45% of the time, Pallas kernels for 0%

profile of v1, /device:TPU:0, one launch (start us, length us, event | category | flops | bytes accessed | tf_op | source)
XLA Modules:
  0.0 834.5 jit_solution(8815689208058110638)
XLA Ops:
  22.4 22.0 %all_gather.3 = bf16[2,2048]{1,0:T(2,128)(2,1)S(1)} all-gather(bf16[2,256]{1,0:T(2,128)(2,1)S(1)} %pad_maximum_fusion.22), channel_id=1, replica_groups=mesh['dp'=4,'sp'=8] {'sp'}, dimensions={1}, use_global_device_ids=true | all-gather | bytes 9216 | tf_op jit(solution)/shard_map/all_gather | solution.py:440
  90.4 10.7 %collective-permute-done.97 = bf16[128,2048]{1,0:T(8,128)(2,1)} collective-permute-done((bf16[128,2048]{1,0:T(8,128)(2,1)}, bf16[128,2048]{1,0:T(8,128)(2,1)}, u32[]{:S(2)}, u32[]{:S(2)}) %collective-permute-start.97) | collective-permute-done | bytes 524320 | tf_op jit(solution)/shard_map/ppermute | solution.py:263
  114.8 7.9 collective-permute-done.79
  169.6 14.7 %while.140 = (s32[]{:T(128)}, bf16[1024,256]{0,1:T(8,128)(2,1)S(1)}, f32[4,1024]{1,0:T(4,128)}, bf16[1024,256]{0,1:T(8,128)(2,1)S(1)}, s32[1024]{0:T(1024)S(1)},...) while((s32[]{:T(128)}, bf16[1024,256]{0,1:T(8,128)(2,1)S(1)}, ...), condition=%wide.region_11.12_spmd, body=%wide.region_4.11_spmd.sunk | while | flops 416030720 | bytes 14422893 | solution.py:161
  212.8 8.3 fusion.213
  241.8 20.5 %collective-permute-done.87 = bf16[128,2048]{1,0:T(8,128)(2,1)S(1)} collective-permute-done((bf16[128,2048]{1,0:T(8,128)(2,1)S(1)}, bf16[128,2048]{1,0:T(8,128)(2,1)S(1)}, u32[]{:S(2)}, u32[]{:S(2)}) %collective-permute-start.87) | collective-permute-done | bytes 524320 | tf_op jit(solution)/shard_map/ppermute | solution.py:263
  262.3 9.5 %collective-permute-start.15 = (bf16[64,2048]{1,0:T(8,128)(2,1)S(1)}, bf16[64,2048]{1,0:T(8,128)(2,1)S(1)}, u32[]{:S(2)}, u32[]{:S(2)}) collective-permute-start(bf16[64,2048]{1,0:T(8,128)(2,1)S(1)} %slice.395), channel_id=1, source_target_pairs={{0,4},{1,5},{2,6},{3,7},{4,0},{5,1},{6,2},{7,3},{8,12},{9,13},{10,... | collective-permute-start | bytes 786440 | tf_op jit(solution)/shard_map/ppermute | solution.py:263
  281.3 12.2 %collective-permute-done.106 = bf16[128,2048]{1,0:T(8,128)(2,1)S(1)} collective-permute-done((bf16[128,2048]{1,0:T(8,128)(2,1)S(1)}, bf16[128,2048]{1,0:T(8,128)(2,1)S(1)}, u32[]{:S(2)}, u32[]{:S(2)}) %collective-permute-start.106) | collective-permute-done | bytes 524320 | tf_op jit(solution)/shard_map/ppermute | solution.py:263
  328.0 11.3 %multiply_convert_fusion.9 = (bf16[1024,1024]{1,0:T(8,128)(2,1)}, bf16[1024,1024]{1,0:T(8,128)(2,1)}, bf16[1024,1024]{1,0:T(8,128)(2,1)}) fusion(f32[1024,1024]{1,0:T(8,128)} %fusion.203, f32[1024,1024]{1,0:T(8,128)} %fusion.204, bf16[1024,2048]{1,0:T(8,128)(2,1)S(1)} %copy-done.50, bf16[1024,2048]{1,0:T(8,128)(2,1)} %param.36), kind=kOutput, calls=%fused_computation.106 | convolution fusion | flops 4310695936 | bytes 23068672 | tf_op jit(solution)/shard_map/dot_general | solution.py:63
  384.4 9.0 %collective-permute-done.109 = bf16[64,2048]{1,0:T(8,128)(2,1)S(1)} collective-permute-done((bf16[64,2048]{1,0:T(8,128)(2,1)S(1)}, bf16[64,2048]{1,0:T(8,128)(2,1)S(1)}, u32[]{:S(2)}, u32[]{:S(2)}) %collective-permute-start.109) | collective-permute-done | bytes 262176 | tf_op jit(solution)/shard_map/ppermute | solution.py:263
  449.4 12.1 %fusion.64 = f32[2048,1024]{1,0:T(8,128)} fusion(bf16[1024,2048]{1,0:T(8,128)(2,1)S(1)} %constant_dynamic-update-slice_fusion.71, f32[1024,1024]{1,0:T(8,128)} %fusion.207, f32[1024,1024]{1,0:T(8,128)} %fusion.209), kind=kOutput, calls=%fused_computation.119 | convolution fusion | flops 4301258752 | bytes 20971520 | tf_op jit(solution)/shard_map/dot_general | solution.py:63
  461.5 12.0 %fusion.61 = f32[2048,1024]{1,0:T(8,128)} fusion(bf16[1024,2048]{1,0:T(8,128)(2,1)S(1)} %constant_dynamic-update-slice_fusion.71, f32[1024,1024]{1,0:T(8,128)} %fusion.209, f32[1024,1024]{1,0:T(8,128)} %fusion.207, f32[1024,1024]{1,0:T(8,128)} %fusion.208), kind=kOutput, calls=%fused_computation.116 | convolution fusion | flops 4305453056 | bytes 25165824 | tf_op jit(solution)/shard_map/dot_general | solution.py:63
  473.6 9.6 %fusion.65 = f32[2048,1024]{1,0:T(8,128)} fusion(bf16[1024,2048]{1,0:T(8,128)(2,1)S(1)} %constant_dynamic-update-slice_fusion.89, f32[1024,1024]{1,0:T(8,128)} %fusion.210, f32[1024,1024]{1,0:T(8,128)S(1)} %fusion.212), kind=kOutput, calls=%fused_computation.120 | convolution fusion | flops 4301258752 | bytes 20971520 | tf_op jit(solution)/shard_map/dot_general | solution.py:63
  490.9 19.8 %add_add_fusion.1 = f32[2048,1024]{1,0:T(8,128)} fusion(f32[2048,1024]{1,0:T(8,128)} %fusion.65, f32[2048,1024]{1,0:T(8,128)} %fusion.216, f32[2048,1024]{1,0:T(8,128)} %fusion.64, bf16[1024,2048]{1,0:T(8,128)(2,1)} %copy-done.63, f32[1024,1024]{1,0:T(8,128)} %fusion.213, f32[1024,1024]{1,0:T(8,128)S(1)} %fusion.215), kind=kOutput, calls=%fused_computation.86 | convolution fusion | flops 4307550208 | bytes 46137344 | tf_op jit(solution)/shard_map/dot_general | solution.py:63
  510.7 22.0 %add_add_fusion.2 = f32[2048,1024]{1,0:T(8,128)} fusion(f32[2048,1024]{1,0:T(8,128)} %fusion.62, f32[2048,1024]{1,0:T(8,128)} %fusion.206, f32[2048,1024]{1,0:T(8,128)} %fusion.61, bf16[1024,2048]{1,0:T(8,128)(2,1)} %copy-done.63, f32[1024,1024]{1,0:T(8,128)} %copy-done.21, f32[1024,1024]{1,0:T(8,128)} %fusion.213, f32[1024,1024]{1,0:T(8,128)} %fusion.214), kind=kOutput, calls=%fused_computation.87 | convolution fusion | flops 4311744512 | bytes 50331648 | tf_op jit(solution)/shard_map/dot_general | solution.py:63
  532.7 13.1 %fusion.67 = f32[1024,2048]{1,0:T(8,128)} fusion(bf16[1024,2048]{1,0:T(8,128)(2,1)} %copy-done.53, f32[1024,1024]{1,0:T(8,128)} %fusion.208, f32[1024,1024]{1,0:T(8,128)} %fusion.209), kind=kOutput, calls=%fused_computation.122 | convolution fusion | flops 4301258752 | bytes 20971520 | tf_op jit(solution)/shard_map/dot_general | solution.py:63
  577.8 10.1 %collective-permute-done.25 = bf16[128,2048]{1,0:T(8,128)(2,1)S(1)} collective-permute-done((bf16[128,2048]{1,0:T(8,128)(2,1)S(1)}, bf16[128,2048]{1,0:T(8,128)(2,1)S(1)}, u32[]{:S(2)}, u32[]{:S(2)}) %collective-permute-start.25) | collective-permute-done | bytes 524320 | tf_op jit(solution)/shard_map/ppermute | solution.py:263
  594.1 19.3 %add_add_fusion = f32[1024,2048]{1,0:T(8,128)} fusion(f32[1024,2048]{1,0:T(8,128)} %fusion.68, f32[1024,2048]{1,0:T(8,128)} %fusion.217, f32[1024,2048]{1,0:T(8,128)} %fusion.67, bf16[1024,2048]{1,0:T(8,128)(2,1)} %constant_dynamic-update-slice_fusion.116, f32[1024,1024]{1,0:T(8,128)} %fusion.214, f32[1024,1024]{1,0:T(8,128)S(1)} %copy-done.22), kind=kOutput, calls=%fused_computation.85 | convolution fusion | flops 4307550208 | bytes 46137344 | tf_op jit(solution)/shard_map/dot_general | solution.py:63
  637.3 29.8 %while.143 = (s32[]{:T(128)}, bf16[1024,256]{0,1:T(8,128)(2,1)S(1)}, f32[1024,1,64]{0,2,1:T(8,128)S(1)}, f32[1024,1,64]{0,2,1:T(8,128)}, bf16[1024,256]{0,1:T(8,...) while((s32[]{:T(128)}, bf16[1024,256]{0,1:T(8,128)(2,1)S(1)}, ...), condition=%wide.region_22.23_spmd, body=%wide.region_15.22_spmd.sunk | while | flops 957515776 | bytes 40563820 | solution.py:253
  656.3 10.5 %while.147 = (s32[]{:T(128)}, f32[512,4,64]{0,2,1:T(8,128)S(1)}, f32[1024,1,64]{0,2,1:T(8,128)S(1)}, f32[1024,1,64]{0,2,1:T(8,128)}, s32[]{:T(128)}, /*index=5*/...) while((s32[]{:T(128)}, f32[512,4,64]{0,2,1:T(8,128)S(1)}, ...), condition=%wide.region_21.21_spmd.clone, body=%wide.region_19.20_spmd.clone.sunk | while | flops 682918912 | bytes 26190144 | solution.py:234
  695.6 9.0 %collective-permute-done.59 = bf16[64,2048]{1,0:T(8,128)(2,1)S(1)} collective-permute-done((bf16[64,2048]{1,0:T(8,128)(2,1)S(1)}, bf16[64,2048]{1,0:T(8,128)(2,1)S(1)}, u32[]{:S(2)}, u32[]{:S(2)}) %collective-permute-start.59) | collective-permute-done | bytes 262176 | tf_op jit(solution)/shard_map/ppermute | solution.py:263
  710.9 24.6 %collective-permute-done.53 = bf16[8,64,384]{2,1,0:T(8,128)(2,1)S(1)} collective-permute-done((bf16[8,64,384]{2,1,0:T(8,128)(2,1)S(1)}, bf16[8,64,384]{2,1,0:T(8,128)(2,1)S(1)}, u32[]{:S(2)}, u32[]{:S(2)}) %collective-permute-start.53) | collective-permute-done | bytes 393248 | tf_op jit(solution)/shard_map/ppermute | solution.py:263
  744.5 10.8 %collective-permute-done.62 = bf16[64,2048]{1,0:T(8,128)(2,1)} collective-permute-done((bf16[64,2048]{1,0:T(8,128)(2,1)}, bf16[64,2048]{1,0:T(8,128)(2,1)}, u32[]{:S(2)}, u32[]{:S(2)}) %collective-permute-start.62) | collective-permute-done | bytes 262176 | tf_op jit(solution)/shard_map/ppermute | solution.py:263
  786.6 19.9 %collective-permute-done.56 = bf16[8,64,384]{2,0,1:T(8,128)(2,1)S(1)} collective-permute-done((bf16[8,64,384]{2,0,1:T(8,128)(2,1)S(1)}, bf16[8,64,384]{2,0,1:T(8,128)(2,1)S(1)}, u32[]{:S(2)}, u32[]{:S(2)}) %collective-permute-start.56) | collective-permute-done | bytes 393248 | tf_op jit(solution)/shard_map/ppermute | solution.py:263
  (856 shorter events, 556.0 us)
Async XLA Ops:
  0.7 59.0 %collective-permute-start.1 = (bf16[128,2048]{1,0:T(8,128)(2,1)}, bf16[128,2048]{1,0:T(8,128)(2,1)}, u32[]{:S(2)}, u32[]{:S(2)}) collective-permute-start(bf16[128,2048]{1,0:T(8,128)(2,1)} %param.26), channel_id=1, source_target_pairs={{0,4},{1,5},{2,6},{3,7},{4,0},{5,1},{6,2},{7,3},{8,12},{9,13},{10,... | collective-permute-start | bytes 1572872 | tf_op jit(solution)/shard_map/ppermute | solution.py:263
  3.7 57.3 %collective-permute-start = (bf16[128,2048]{1,0:T(8,128)(2,1)}, bf16[128,2048]{1,0:T(8,128)(2,1)}, u32[]{:S(2)}, u32[]{:S(2)}) collective-permute-start(bf16[128,2048]{1,0:T(8,128)(2,1)} %param.26), channel_id=1, source_target_pairs={{0,2},{1,3},{2,0},{3,1},{4,6},{5,7},{6,4},{7,5},{8,10},{9,11},{10,... | collective-permute-start | bytes 1572872 | tf_op jit(solution)/shard_map/ppermute | solution.py:263
  5.2 52.9 %collective-permute-start.78 = (bf16[128,2048]{1,0:T(8,128)(2,1)}, bf16[128,2048]{1,0:T(8,128)(2,1)}, u32[]{:S(2)}, u32[]{:S(2)}) collective-permute-start(bf16[128,2048]{1,0:T(8,128)(2,1)} %param.37), channel_id=1, source_target_pairs={{0,8},{8,0},{16,24},{24,16},{1,9},{9,1},{17,25},{25,17},{2,10},{10... | collective-permute-start | bytes 1572872 | tf_op jit(solution)/shard_map/ppermute | solution.py:263
  6.8 49.3 %collective-permute-start.114 = (bf16[128,2048]{1,0:T(8,128)(2,1)}, bf16[128,2048]{1,0:T(8,128)(2,1)}, u32[]{:S(2)}, u32[]{:S(2)}) collective-permute-start(bf16[128,2048]{1,0:T(8,128)(2,1)} %param.37), channel_id=1, source_target_pairs={{0,24},{8,16},{16,8},{24,0},{1,25},{9,17},{17,9},{25,1},{2,26},{10... | collective-permute-start | bytes 1572872 | tf_op jit(solution)/shard_map/ppermute | solution.py:263
  9.2 45.2 %collective-permute-start.96 = (bf16[128,2048]{1,0:T(8,128)(2,1)}, bf16[128,2048]{1,0:T(8,128)(2,1)}, u32[]{:S(2)}, u32[]{:S(2)}) collective-permute-start(bf16[128,2048]{1,0:T(8,128)(2,1)} %param.37), channel_id=1, source_target_pairs={{0,16},{8,24},{16,0},{24,8},{1,17},{9,25},{17,1},{25,9},{2,18},{10... | collective-permute-start | bytes 1572872 | tf_op jit(solution)/shard_map/ppermute | solution.py:263
  16.1 144.4 %all-to-all-start = ((bf16[8,256,384]{1,2,0:T(8,128)(2,1)}), bf16[8,256,384]{1,2,0:T(8,128)(2,1)}, u32[]{:S(2)}, u32[]{:S(2)}) async-start(bf16[8,256,384]{1,2,0:T(8,128)(2,1)} %maximum_bitcast_fusion), calls=%async_computation | async-start | bytes 3145728 | tf_op jit(solution)/shard_map/all_to_all | solution.py:437
  78.4 48.5 %collective-permute-start.6 = (bf16[128,2048]{1,0:T(8,128)(2,1)}, bf16[128,2048]{1,0:T(8,128)(2,1)S(1)}, u32[]{:S(2)}, u32[]{:S(2)}) collective-permute-start(bf16[128,2048]{1,0:T(8,128)(2,1)} %collective-permute-done.1), channel_id=1, source_target_pairs={{0,1},{1,0},{2,3},{3,2},{4,5},{5,4},{6,7},{7,6},{8,9},{9,8},{10,11... | collective-permute-start | bytes 1572872 | tf_op jit(solution)/shard_map/ppermute | solution.py:263
  83.6 42.6 %collective-permute-start.5 = (bf16[128,2048]{1,0:T(8,128)(2,1)}, bf16[128,2048]{1,0:T(8,128)(2,1)S(1)}, u32[]{:S(2)}, u32[]{:S(2)}) collective-permute-start(bf16[128,2048]{1,0:T(8,128)(2,1)} %collective-permute-done), channel_id=1, source_target_pairs={{0,1},{1,0},{2,3},{3,2},{4,5},{5,4},{6,7},{7,6},{8,9},{9,8},{10,11... | collective-permute-start | bytes 1572872 | tf_op jit(solution)/shard_map/ppermute | solution.py:263
  113.9 72.4 %collective-permute-start.83 = (bf16[128,2048]{1,0:T(8,128)(2,1)}, bf16[128,2048]{1,0:T(8,128)(2,1)}, u32[]{:S(2)}, u32[]{:S(2)}) collective-permute-start(bf16[128,2048]{1,0:T(8,128)(2,1)} %collective-permute-done.78), channel_id=1, source_target_pairs={{0,1},{1,0},{2,3},{3,2},{4,5},{5,4},{6,7},{7,6},{8,9},{9,8},{10,11... | collective-permute-start | bytes 1572872 | tf_op jit(solution)/shard_map/ppermute | solution.py:263
  156.1 42.0 %collective-permute-start.85 = (bf16[128,2048]{1,0:T(8,128)(2,1)}, bf16[128,2048]{1,0:T(8,128)(2,1)}, u32[]{:S(2)}, u32[]{:S(2)}) collective-permute-start(bf16[128,2048]{1,0:T(8,128)(2,1)} %collective-permute-done.80), channel_id=1, source_target_pairs={{0,1},{1,0},{2,3},{3,2},{4,5},{5,4},{6,7},{7,6},{8,9},{9,8},{10,11... | collective-permute-start | bytes 1572872 | tf_op jit(solution)/shard_map/ppermute | solution.py:263
  157.6 35.8 %collective-permute-start.103 = (bf16[128,2048]{1,0:T(8,128)(2,1)}, bf16[128,2048]{1,0:T(8,128)(2,1)}, u32[]{:S(2)}, u32[]{:S(2)}) collective-permute-start(bf16[128,2048]{1,0:T(8,128)(2,1)} %collective-permute-done.98), channel_id=1, source_target_pairs={{0,1},{1,0},{2,3},{3,2},{4,5},{5,4},{6,7},{7,6},{8,9},{9,8},{10,11... | collective-permute-start | bytes 1572872 | tf_op jit(solution)/shard_map/ppermute | solution.py:263
  240.1 41.1 %collective-permute-start.17 = (bf16[128,2048]{1,0:T(8,128)(2,1)S(1)}, bf16[128,2048]{1,0:T(8,128)(2,1)S(1)}, u32[]{:S(2)}, u32[]{:S(2)}) collective-permute-start(bf16[128,2048]{1,0:T(8,128)(2,1)S(1)} %get-tuple-element.999), channel_id=1, source_target_pairs={{0,1},{1,0},{2,3},{3,2},{4,5},{5,4},{6,7},{7,6},{8,9},{9,8},{10,11... | collective-permute-start | bytes 1572872 | tf_op jit(solution)/shard_map/ppermute | solution.py:263
  271.9 138.5 %collective-permute-start.92 = (bf16[128,2048]{1,0:T(8,128)(2,1)S(1)}, bf16[128,2048]{1,0:T(8,128)(2,1)S(1)}, u32[]{:S(2)}, u32[]{:S(2)}) collective-permute-start(bf16[128,2048]{1,0:T(8,128)(2,1)S(1)} %collective-permute-done.87), channel_id=1, source_target_pairs={{0,1},{1,0},{2,3},{3,2},{4,5},{5,4},{6,7},{7,6},{8,9},{9,8},{10,11... | collective-permute-start | bytes 1572872 | tf_op jit(solution)/shard_map/ppermute | solution.py:263
  272.0 39.7 %collective-permute-start.89 = (bf16[128,2048]{1,0:T(8,128)(2,1)S(1)}, bf16[128,2048]{1,0:T(8,128)(2,1)S(1)}, u32[]{:S(2)}, u32[]{:S(2)}) collective-permute-start(bf16[128,2048]{1,0:T(8,128)(2,1)S(1)} %collective-permute-done.87), channel_id=1, source_target_pairs={{0,4},{1,5},{2,6},{3,7},{4,0},{5,1},{6,2},{7,3},{8,12},{9,13},{10,... | collective-permute-start | bytes 1572872 | tf_op jit(solution)/shard_map/ppermute | solution.py:263
  303.6 106.7 %collective-permute-start.74 = (bf16[128,2048]{1,0:T(8,128)(2,1)S(1)}, bf16[128,2048]{1,0:T(8,128)(2,1)S(1)}, u32[]{:S(2)}, u32[]{:S(2)}) collective-permute-start(bf16[128,2048]{1,0:T(8,128)(2,1)S(1)} %collective-permute-done.69), channel_id=1, source_target_pairs={{0,1},{1,0},{2,3},{3,2},{4,5},{5,4},{6,7},{7,6},{8,9},{9,8},{10,11... | collective-permute-start | bytes 1572872 | tf_op jit(solution)/shard_map/ppermute | solution.py:263
  312.5 92.9 %collective-permute-start.110 = (bf16[128,2048]{1,0:T(8,128)(2,1)S(1)}, bf16[128,2048]{1,0:T(8,128)(2,1)S(1)}, u32[]{:S(2)}, u32[]{:S(2)}) collective-permute-start(bf16[128,2048]{1,0:T(8,128)(2,1)S(1)} %collective-permute-done.105), channel_id=1, source_target_pairs={{0,1},{1,0},{2,3},{3,2},{4,5},{5,4},{6,7},{7,6},{8,9},{9,8},{10,11... | collective-permute-start | bytes 1572872 | tf_op jit(solution)/shard_map/ppermute | solution.py:263
  313.5 61.8 %collective-permute-start.72 = (bf16[64,2048]{1,0:T(8,128)(2,1)S(1)}, bf16[64,2048]{1,0:T(8,128)(2,1)S(1)}, u32[]{:S(2)}, u32[]{:S(2)}) collective-permute-start(bf16[64,2048]{1,0:T(8,128)(2,1)S(1)} %slice.437), channel_id=1, source_target_pairs={{0,4},{1,5},{2,6},{3,7},{4,0},{5,1},{6,2},{7,3},{8,12},{9,13},{10,... | collective-permute-start | bytes 786440 | tf_op jit(solution)/shard_map/ppermute | solution.py:263
  314.6 58.6 %collective-permute-start.108 = (bf16[64,2048]{1,0:T(8,128)(2,1)S(1)}, bf16[64,2048]{1,0:T(8,128)(2,1)S(1)}, u32[]{:S(2)}, u32[]{:S(2)}) collective-permute-start(bf16[64,2048]{1,0:T(8,128)(2,1)S(1)} %slice.445), channel_id=1, source_target_pairs={{0,4},{1,5},{2,6},{3,7},{4,0},{5,1},{6,2},{7,3},{8,12},{9,13},{10,... | collective-permute-start | bytes 786440 | tf_op jit(solution)/shard_map/ppermute | solution.py:263
  414.3 138.4 %collective-permute-start.21 = (bf16[512,2048]{1,0:T(8,128)(2,1)}, bf16[512,2048]{1,0:T(8,128)(2,1)}, u32[]{:S(2)}, u32[]{:S(2)}) collective-permute-start(bf16[512,2048]{1,0:T(8,128)(2,1)} %convolution_convert_fusion), channel_id=1, source_target_pairs={{0,1},{1,0},{2,3},{3,2},{4,5},{5,4},{6,7},{7,6},{8,9},{9,8},{10,11... | collective-permute-start | bytes 6291464 | tf_op jit(solution)/shard_map/ppermute | solution.py:263
  414.8 131.0 %collective-permute-start.34 = (bf16[512,2048]{1,0:T(8,128)(2,1)}, bf16[512,2048]{1,0:T(8,128)(2,1)}, u32[]{:S(2)}, u32[]{:S(2)}) collective-permute-start(bf16[512,2048]{1,0:T(8,128)(2,1)} %add_convert_fusion), channel_id=1, source_target_pairs={{0,1},{1,0},{2,3},{3,2},{4,5},{5,4},{6,7},{7,6},{8,9},{9,8},{10,11... | collective-permute-start | bytes 6291464 | tf_op jit(solution)/shard_map/ppermute | solution.py:263
  685.8 71.1 %collective-permute-start.47 = (bf16[512,2048]{1,0:T(8,128)(2,1)}, bf16[512,2048]{1,0:T(8,128)(2,1)}, u32[]{:S(2)}, u32[]{:S(2)}) collective-permute-start(bf16[512,2048]{1,0:T(8,128)(2,1)} %convolution_convert_fusion.2), channel_id=1, source_target_pairs={{0,1},{1,0},{2,3},{3,2},{4,5},{5,4},{6,7},{7,6},{8,9},{9,8},{10,11... | collective-permute-start | bytes 6291464 | tf_op jit(solution)/shard_map/ppermute | solution.py:263
  690.7 44.7 %collective-permute-start.53 = (bf16[8,64,384]{2,1,0:T(8,128)(2,1)S(1)}, bf16[8,64,384]{2,1,0:T(8,128)(2,1)S(1)}, u32[]{:S(2)}, u32[]{:S(2)}) collective-permute-start(bf16[8,64,384]{2,1,0:T(8,128)(2,1)S(1)} %get-tuple-element.1032), channel_id=1, source_target_pairs={{0,16},{8,24},{16,0},{24,8},{1,17},{9,25},{17,1},{25,9},{2,18},{10... | collective-permute-start | bytes 1179656 | tf_op jit(solution)/shard_map/ppermute | solution.py:263
  694.4 43.7 %collective-permute-start.54 = (bf16[8,64,384]{2,1,0:T(8,128)(2,1)S(1)}, bf16[8,64,384]{2,1,0:T(8,128)(2,1)S(1)}, u32[]{:S(2)}, u32[]{:S(2)}) collective-permute-start(bf16[8,64,384]{2,1,0:T(8,128)(2,1)S(1)} %get-tuple-element.1033), channel_id=1, source_target_pairs={{0,24},{8,16},{16,8},{24,0},{1,25},{9,17},{17,9},{25,1},{2,26},{10... | collective-permute-start | bytes 1179656 | tf_op jit(solution)/shard_map/ppermute | solution.py:263
  706.6 48.6 %collective-permute-start.62 = (bf16[64,2048]{1,0:T(8,128)(2,1)}, bf16[64,2048]{1,0:T(8,128)(2,1)}, u32[]{:S(2)}, u32[]{:S(2)}) collective-permute-start(bf16[64,2048]{1,0:T(8,128)(2,1)} %get-tuple-element.962), channel_id=1, source_target_pairs={{0,16},{8,24},{16,0},{24,8},{1,17},{9,25},{17,1},{25,9},{2,18},{10... | collective-permute-start | bytes 786440 | tf_op jit(solution)/shard_map/ppermute | solution.py:263
  (204 other events, 2813.7 us)
